TPU v7x, 128 devices: a whole 4x4x4 slice. The times are simulated.
128 devices in a mesh: ax: 16 (over z, y), az: 8 (over x, core).
Axes of the slice: x: 4, y: 4, z: 4, core: 2. Of those that a mesh axis runs over, the one named last changes fastest.
Arguments:
- lamb_vector: bfloat16 [32768, 3, 512], P(('ax', 'az')), may hold values from -6 to 6
- owner: int32 [32768, 1], P(('ax', 'az')), may hold values from 0 to 127; in each aligned block of 256 rows (0 to 255, 256 to 511, ...) at most 6 rows name the same one
- element: int32 [32768], P(('ax', 'az')), may hold values from 0 to 1023
- shape_class: int32 [32768], P(('ax', 'az')), may hold values from 0 to 1
- interp_tables: bfloat16 [2, 512, 125], replicated, may hold values from -0.25 to 0.25
- acoustic_state: float32 [5, 125, 32, 32, 128], P(None, None, 'ax', 'az'), may hold values from -6 to 6
Outputs:
- new_state: float32 [5, 125, 32, 32, 128], P(None, None, 'ax', 'az')
- source: float32 [3, 125, 32, 32, 128], P(None, None, 'ax', 'az')
Inputs may be any that keep to these rules, and one draw needn't show every extreme that they name: `owner`: among one device's 256 flow elements no device is named by more than 6 of them, and some device is named by exactly 6.
All inputs are finite; a program needn't handle non-finite values.
Results may differ from a plain program's by a relative error of at most 0.0013.
Values may be sent and summed in bfloat16 or wider, within the bound.
A program may use at most 128 MiB of HBM per device.

v0:
```python
import functools
import math

import jax
import jax.numpy as jnp
import numpy as np
from jax import lax
from jax.experimental import pallas as pl
from jax.experimental.pallas import tpu as pltpu
from jax.sharding import PartitionSpec as P

MACH = 0.3
SPEED = 1.3
DT = 0.03
LIFT = 10.0
VOLUME = 2.0
SLOTS = 6
MESH = pl.DeviceIdType.MESH
F32 = jnp.float32
BF16 = jnp.bfloat16


def line_matrix():
    points = [-1.0, -math.sqrt(3.0 / 7.0), 0.0, math.sqrt(3.0 / 7.0), 1.0]
    bary = [
        1.0 / math.prod(points[c] - points[o] for o in range(5) if o != c) for c in range(5)
    ]
    d = np.zeros((5, 5))
    for i in range(5):
        for j in range(5):
            if i != j:
                d[i, j] = bary[j] / bary[i] / (points[i] - points[j])
        d[i, i] = -np.sum(d[i])
    return -VOLUME * d


D = line_matrix()


def deriv(x):
    e0, e1, o0, o1 = x[0] + x[4], x[1] + x[3], x[0] - x[4], x[1] - x[3]
    y = [None] * 5
    for i in range(2):
        odd = float(0.5 * (D[i, 0] - D[i, 4])) * o0 + float(0.5 * (D[i, 1] - D[i, 3])) * o1
        even = (
            float(0.5 * (D[i, 0] + D[i, 4])) * e0
            + float(0.5 * (D[i, 1] + D[i, 3])) * e1
            + float(D[i, 2]) * x[2]
        )
        y[i], y[4 - i] = odd + even, odd - even
    y[2] = float(D[2, 0]) * o0 + float(D[2, 1]) * o1
    return y


def cross_terms(jump, normal, along):
    t = (LIFT * normal) * jump[along]
    out = [None] * 5
    for f in (0, 4):
        out[f] = t - (LIFT * SPEED) * jump[f]
    for f in (1, 2, 3):
        out[f] = (-LIFT * SPEED) * jump[f]
    g = MACH * jump[1] + jump[0]
    out[along] = out[along] + (LIFT * normal) * g
    return out


def axial_terms(jump, normal):
    p, u, v, w, d = jump
    near = LIFT * (normal * MACH - SPEED)
    t = (LIFT * normal) * u
    return [
        near * p + t,
        near * u + (LIFT * normal) * p,
        (-LIFT * SPEED) * v,
        (-LIFT * SPEED) * w,
        near * d + t,
    ]


def kernel(
    nax, naz,
    state_hbm, lamb_ref, table_ref, owner_ref, element_ref, class_ref,
    new_hbm, source_hbm,
    q_ref, bufs, acc, s_ref, post, inbox,
    xs, xl, xr, ys, yl, yr,
    state_sem, self_sem, mail_send, mail_recv, xsend, xrecv, ysend, yrecv, out_sem,
):
    n = nax * naz
    ax, az = lax.axis_index("ax"), lax.axis_index("az")
    me = ax * naz + az
    has_left, has_right = ax > 0, ax < nax - 1
    az_up, az_down = lax.rem(az + 1, naz), lax.rem(az + naz - 1, naz)
    row = lax.broadcasted_iota(jnp.int32, (8, 128), 0)
    lane = lax.broadcasted_iota(jnp.int32, (8, 128), 1)
    low_half = row < 4
    ey = row & 3

    load_state = pltpu.make_async_copy(state_hbm, q_ref, state_sem)
    load_state.start()

    def clear(i, carry):
        inbox[i] = jnp.zeros(inbox.shape[1:], F32)
        return carry

    lax.fori_loop(0, n, clear, 0)

    @pl.when(jnp.logical_not(has_left))
    def _():
        def body(i, carry):
            for k in range(4):
                xl[k, i] = jnp.zeros(xl.shape[2:], BF16)
            return carry
        lax.fori_loop(0, 5, body, 0)

    @pl.when(jnp.logical_not(has_right))
    def _():
        def body(i, carry):
            for k in range(4):
                xr[k, i] = jnp.zeros(xr.shape[2:], BF16)
            return carry
        lax.fori_loop(0, 5, body, 0)

    barrier = pltpu.get_barrier_semaphore()

    def greet(i, carry):
        other = lax.rem(me + i, n)
        pl.semaphore_signal(
            barrier, inc=1, device_id=(other // naz, lax.rem(other, naz)), device_id_type=MESH
        )
        return carry

    lax.fori_loop(1, n, greet, 0)

    owner, element, shape_class = owner_ref[...], element_ref[...], class_ref[...]
    count = owner.shape[1]
    hit = lax.broadcasted_iota(jnp.int32, (n, count), 0) == owner
    hit = jnp.where(hit, 1.0, 0.0)
    earlier = lax.broadcasted_iota(jnp.int32, (count, count), 0) < lax.broadcasted_iota(
        jnp.int32, (count, count), 1
    )
    ranks = jnp.dot(
        hit.astype(BF16), jnp.where(earlier, 1.0, 0.0).astype(BF16), preferred_element_type=F32
    )
    position = jnp.sum(hit * ranks, axis=0, keepdims=True).astype(jnp.int32)
    slot = owner * 8 + position
    place = lax.broadcasted_iota(jnp.int32, (n * 8, count), 0) == slot
    place = jnp.where(place, 1.0, 0.0).astype(BF16)
    node_row = lax.broadcasted_iota(jnp.int32, (128, count), 0)
    for c in range(3):
        both = lax.dot_general(
            table_ref[...], lamb_ref[c], (((1,), (1,)), ((), ())), preferred_element_type=F32
        )
        value = jnp.where(shape_class == 0, both[:128], both[128:])
        if c == 0:
            value = jnp.where(node_row == 125, ((element >> 5) + 1).astype(F32), value)
            value = jnp.where(node_row == 126, (element & 31).astype(F32), value)
        high = value.astype(BF16)
        low = (value - high.astype(F32)).astype(BF16)
        mail = lax.dot_general(
            place, jnp.concatenate([high, low], axis=0), (((1,), (1,)), ((), ())),
            preferred_element_type=F32,
        )
        post[:, c] = (mail[:, :128] + mail[:, 128:]).reshape(n, 8, 128)

    def x_copy(k, b, side):
        if side == 0:
            dst, dev = xl, (ax + 1, az)
        else:
            dst, dev = xr, (ax - 1, az)
        return pltpu.make_async_remote_copy(
            src_ref=xs.at[k, b, side], dst_ref=dst.at[k, b], send_sem=xsend.at[k, b, side],
            recv_sem=xrecv.at[k, b, side], device_id=dev, device_id_type=MESH,
        )

    def y_copy(k, side):
        if side == 0:
            dst, dev = yl, (ax, az_up)
        else:
            dst, dev = yr, (ax, az_down)
        return pltpu.make_async_remote_copy(
            src_ref=ys.at[k, side], dst_ref=dst.at[k], send_sem=ysend.at[k, side],
            recv_sem=yrecv.at[k, side], device_id=dev, device_id_type=MESH,
        )

    def pack_x(ref, k, b):
        for side in range(2):
            a = 4 if side == 0 else 0
            parts = []
            for m in range(14):
                pair = []
                for q in (2 * m, 2 * m + 1):
                    pair.append(ref[q % 5, a, b, q // 5] if q < 25 else jnp.zeros((8, 128), F32))
                even, odd = pltpu.roll(pair[0], 4, 0), pair[1]
                parts.append(
                    jnp.where(low_half, even, odd) if side == 0 else jnp.where(low_half, odd, even)
                )
            for t in range(7):
                xs[k, b, side, 16 * t:16 * t + 16, :] = jnp.concatenate(
                    [parts[2 * t], parts[2 * t + 1]], axis=0
                ).astype(BF16)

    def pack_y(ref, k, side):
        b = 4 if side == 0 else 0

        def body(a, carry):
            parts = []
            for m in range(8):
                total = jnp.zeros((8, 128), F32)
                for j in range(4):
                    q = 4 * m + j
                    if q < 25:
                        turn = (j - 3) % 8 if side == 0 else (3 + j) % 8
                        value = ref[q % 5, a, b, q // 5]
                        value = pltpu.roll(value, turn, 0) if turn else value
                        residue = j if side == 0 else (3 + j) % 4
                        total = jnp.where(ey == residue, value, total)
                parts.append(total)
            for t in range(4):
                ys[k, side, a, 16 * t:16 * t + 16, :] = jnp.concatenate(
                    [parts[2 * t], parts[2 * t + 1]], axis=0
                ).astype(BF16)
            return carry

        lax.fori_loop(0, 5, body, 0)

    def send_x(k, b):
        @pl.when(has_right)
        def _():
            x_copy(k, b, 0).start()

        @pl.when(has_left)
        def _():
            x_copy(k, b, 1).start()

    load_state.wait()

    def first_x(b, carry):
        pack_x(q_ref, 0, b)
        return carry

    lax.fori_loop(0, 5, first_x, 0)
    pack_y(q_ref, 0, 0)
    pack_y(q_ref, 0, 1)

    pl.semaphore_wait(barrier, n - 1)

    y_copy(0, 0).start()
    y_copy(0, 1).start()

    def first_send(b, carry):
        send_x(0, b)
        return carry

    lax.fori_loop(0, 5, first_send, 0)

    def mail_copy(other):
        return pltpu.make_async_remote_copy(
            src_ref=post.at[other, :, pl.ds(0, SLOTS)], dst_ref=inbox.at[me, :, pl.ds(0, SLOTS)],
            send_sem=mail_send, recv_sem=mail_recv,
            device_id=(other // naz, lax.rem(other, naz)), device_id_type=MESH,
        )

    def mail_out(i, carry):
        mail_copy(lax.rem(me + i, n)).start()
        return carry

    lax.fori_loop(1, n, mail_out, 0)
    inbox[me] = post[me]

    def z_pass(cur, nxt):
        def body(a, carry):
            for b in range(5):
                x = [[cur[f, a, b, r] for r in range(5)] for f in range(5)]
                dw = deriv(x[3])
                dg = deriv([MACH * x[1][r] + x[0][r] for r in range(5)])
                lo = cross_terms(
                    [x[f][0] - jnp.where(lane == 0, 0.0, pltpu.roll(x[f][4], 1, 1)) for f in range(5)],
                    -1.0, 3,
                )
                hi = cross_terms(
                    [x[f][4] - jnp.where(lane == 127, 0.0, pltpu.roll(x[f][0], 127, 1)) for f in range(5)],
                    1.0, 3,
                )
                for r in range(5):
                    for f in range(5):
                        value = dw[r] if f in (0, 4) else dg[r] if f == 3 else None
                        face = lo[f] if r == 0 else hi[f] if r == 4 else None
                        if value is None:
                            value = jnp.zeros((8, 128), F32) if face is None else face
                        elif face is not None:
                            value = value + face
                        nxt[f, a, b, r] = value
            return carry

        lax.fori_loop(0, 5, body, 0)

    def y_pass(cur, nxt, k):
        y_copy(k, 0).wait_recv()
        y_copy(k, 1).wait_recv()

        def body(a, carry):
            down, up = [], []
            for t in range(4):
                wide = yl[k, a, 16 * t:16 * t + 16, :].astype(F32)
                down += [wide[:8], wide[8:]]
                wide = yr[k, a, 16 * t:16 * t + 16, :].astype(F32)
                up += [wide[:8], wide[8:]]
            for r in range(5):
                x = [[cur[f, a, b, r] for b in range(5)] for f in range(5)]
                dv = deriv(x[2])
                dg = deriv([MACH * x[1][b] + x[0][b] for b in range(5)])
                jump_lo, jump_hi = [], []
                for f in range(5):
                    q = 5 * r + f
                    j = q % 4
                    halo = jnp.where(ey == j, down[q // 4], up[q // 4])
                    halo = pltpu.roll(halo, 8 - j, 0) if j else halo
                    jump_lo.append(x[f][0] - jnp.where(ey == 0, halo, pltpu.roll(x[f][4], 1, 0)))
                    jump_hi.append(x[f][4] - jnp.where(ey == 3, halo, pltpu.roll(x[f][0], 7, 0)))
                lo, hi = cross_terms(jump_lo, -1.0, 2), cross_terms(jump_hi, 1.0, 2)
                for b in range(5):
                    for f in range(5):
                        value = dv[b] if f in (0, 4) else dg[b] if f == 2 else None
                        face = lo[f] if b == 0 else hi[f] if b == 4 else None
                        if value is None and face is None:
                            continue
                        if value is None:
                            value = face
                        elif face is not None:
                            value = value + face
                        nxt[f, a, b, r] = nxt[f, a, b, r] + value
            return carry

        lax.fori_loop(0, 5, body, 0)

    def x_pass(cur, nxt, k, scale, first):
        def body(i, carry):
            b = jnp.where(i == 0, 0, jnp.where(i == 1, 4, i - 1))

            @pl.when(has_left)
            def _():
                x_copy(k, b, 0).wait_recv()

            @pl.when(has_right)
            def _():
                x_copy(k, b, 1).wait_recv()

            left, right = [], []
            for t in range(7):
                wide = xl[k, b, 16 * t:16 * t + 16, :].astype(F32)
                left += [wide[:8], wide[8:]]
                wide = xr[k, b, 16 * t:16 * t + 16, :].astype(F32)
                right += [wide[:8], wide[8:]]
            for r in range(5):
                x = [[cur[f, a, b, r] for a in range(5)] for f in range(5)]
                p, u, d = x[0], x[1], x[4]
                diff = {
                    0: deriv([MACH * p[a] + u[a] for a in range(5)]),
                    1: deriv([MACH * u[a] + p[a] for a in range(5)]),
                    4: deriv([MACH * d[a] + u[a] for a in range(5)]),
                }
                jump_lo, jump_hi = [], []
                for f in range(5):
                    q = 5 * r + f
                    m = q // 2
                    if q % 2 == 0:
                        halo = jnp.where(low_half, left[m], right[m])
                    else:
                        halo = pltpu.roll(jnp.where(low_half, right[m], left[m]), 4, 0)
                    own = pltpu.roll(jnp.where(low_half, x[f][4], x[f][0]), 4, 0)
                    jump_lo.append(x[f][0] - jnp.where(low_half, halo, own))
                    jump_hi.append(x[f][4] - jnp.where(low_half, own, halo))
                lo, hi = axial_terms(jump_lo, -1.0), axial_terms(jump_hi, 1.0)
                for a in range(5):
                    for f in range(5):
                        total = nxt[f, a, b, r]
                        if f in diff:
                            total = total + diff[f][a]
                        if a in (0, 4):
                            total = total + (lo[f] if a == 0 else hi[f])
                        if first and f in (1, 2, 3):
                            at = ((f - 1) * 125 + a * 25 + b * 5 + r) * 8
                            total = total + s_ref[pl.ds(pl.multiple_of(at, 8), 8), :]
                        total = scale * total
                        nxt[f, a, b, r] = total
                        before = q_ref[f, a, b, r] if first else acc[f, a, b, r]
                        acc[f, a, b, r] = before + total

            def hand_on():
                pack_x(nxt, k + 1, b)
                send_x(k + 1, b)

                @pl.when(i == 0)
                def _():
                    pack_y(nxt, k + 1, 1)
                    y_copy(k + 1, 1).start()

                @pl.when(i == 1)
                def _():
                    pack_y(nxt, k + 1, 0)
                    y_copy(k + 1, 0).start()

            if first:
                hand_on()
            else:
                pl.when(k < 3)(hand_on)
            return carry

        lax.fori_loop(0, 5, body, 0)

    z_pass(q_ref, bufs.at[0])
    y_pass(q_ref, bufs.at[0], 0)

    arrived = pltpu.make_async_remote_copy(
        src_ref=post.at[pl.ds(0, n - 1), :, pl.ds(0, SLOTS)],
        dst_ref=inbox.at[pl.ds(0, n - 1), :, pl.ds(0, SLOTS)],
        send_sem=mail_send, recv_sem=mail_recv,
        device_id=(ax, az), device_id_type=MESH,
    )
    arrived.wait_recv()
    turned = []
    code = None
    for c in range(3):
        block = inbox[:, c].reshape(n * 8, 128)
        if c == 0:
            code = ((block[:, 125:126] - 1.0) * 32.0 + block[:, 126:127]).astype(jnp.int32)
        turned.append(block.T)
    turned = jnp.concatenate(turned, axis=0)
    high = turned.astype(BF16)
    low = (turned - high.astype(F32)).astype(BF16)

    def spread(t, carry):
        member = code == lax.broadcasted_iota(jnp.int32, (n * 8, 256), 1) + 256 * t
        member = jnp.where(member, 1.0, 0.0).astype(BF16)
        total = jnp.dot(high, member, preferred_element_type=F32)
        total = total + jnp.dot(low, member, preferred_element_type=F32)
        for c in range(3):
            for h in range(2):
                s_ref[pl.ds(c * 1000 + 2 * t + h, 125, stride=8), :] = total[
                    128 * c:128 * c + 125, 128 * h:128 * h + 128
                ]
        return carry

    lax.fori_loop(0, 4, spread, 0)
    save_source = pltpu.make_async_copy(s_ref, source_hbm, out_sem.at[0])
    save_source.start()

    x_pass(q_ref, bufs.at[0], 0, DT, True)

    def stage(k, carry):
        cur, nxt = bufs.at[lax.rem(k + 1, 2)], bufs.at[lax.rem(k, 2)]
        scale = jnp.where(k == 1, DT / 2.0, jnp.where(k == 2, DT / 3.0, DT / 4.0))
        z_pass(cur, nxt)
        y_pass(cur, nxt, k)
        x_pass(cur, nxt, k, scale, False)
        return carry

    lax.fori_loop(1, 4, stage, 0)
    save_new = pltpu.make_async_copy(acc, new_hbm, out_sem.at[1])
    save_new.start()

    arrived.wait_send()

    def drain(k, carry):
        y_copy(k, 0).wait_send()
        y_copy(k, 1).wait_send()

        def inner(b, carry):
            @pl.when(has_right)
            def _():
                x_copy(k, b, 0).wait_send()

            @pl.when(has_left)
            def _():
                x_copy(k, b, 1).wait_send()
            return carry

        lax.fori_loop(0, 5, inner, 0)
        return carry

    lax.fori_loop(0, 4, drain, 0)
    save_source.wait()
    save_new.wait()


def body(nax, naz, lamb_vector, owner, element, shape_class, interp_tables, acoustic_state):
    n = nax * naz
    count = lamb_vector.shape[0]
    lamb = jnp.transpose(lamb_vector, (1, 0, 2))
    table = jnp.pad(jnp.transpose(interp_tables, (0, 2, 1)), ((0, 0), (0, 3), (0, 0)))
    table = table.reshape(256, 512)
    state = acoustic_state.reshape(5, 5, 5, 5, 8, 128)
    vmem, anywhere = pl.BlockSpec(memory_space=pltpu.VMEM), pl.BlockSpec(memory_space=pl.ANY)
    dma = pltpu.SemaphoreType.DMA
    new, source = pl.pallas_call(
        functools.partial(kernel, nax, naz),
        out_shape=(
            jax.ShapeDtypeStruct((5, 5, 5, 5, 8, 128), F32),
            jax.ShapeDtypeStruct((3000, 128), F32),
        ),
        in_specs=[anywhere, vmem, vmem, vmem, vmem, vmem],
        out_specs=(anywhere, anywhere),
        scratch_shapes=[
            pltpu.VMEM((5, 5, 5, 5, 8, 128), F32),
            pltpu.VMEM((2, 5, 5, 5, 5, 8, 128), F32),
            pltpu.VMEM((5, 5, 5, 5, 8, 128), F32),
            pltpu.VMEM((3000, 128), F32),
            pltpu.VMEM((n, 3, 8, 128), F32),
            pltpu.VMEM((n, 3, 8, 128), F32),
            pltpu.VMEM((4, 5, 2, 112, 128), BF16),
            pltpu.VMEM((4, 5, 112, 128), BF16),
            pltpu.VMEM((4, 5, 112, 128), BF16),
            pltpu.VMEM((4, 2, 5, 64, 128), BF16),
            pltpu.VMEM((4, 5, 64, 128), BF16),
            pltpu.VMEM((4, 5, 64, 128), BF16),
            dma, dma, dma, dma,
            dma((4, 5, 2)), dma((4, 5, 2)), dma((4, 2)), dma((4, 2)), dma((2,)),
        ],
        compiler_params=pltpu.CompilerParams(
            collective_id=0, has_side_effects=True, vmem_limit_bytes=50 * 1024 * 1024
        ),
    )(
        state, lamb, table,
        owner.reshape(1, count), element.reshape(1, count), shape_class.reshape(1, count),
    )
    return new.reshape(5, 125, 2, 4, 128), source.reshape(3, 125, 2, 4, 128)


def solution(mesh):
    nax, naz = mesh.shape["ax"], mesh.shape["az"]
    in_specs = (
        P(("ax", "az"), None, None),
        P(("ax", "az"), None),
        P(("ax", "az")),
        P(("ax", "az")),
        P(),
        P(None, None, "ax", "az", None),
    )
    out_specs = (P(None, None, "ax", "az", None), P(None, None, "ax", "az", None))
    return jax.shard_map(
        functools.partial(body, nax, naz), mesh=mesh, in_specs=in_specs, out_specs=out_specs,
        check_vma=False,
    )
```

profile of v0, /device:TPU:32, one launch (start us, length us, event | category | flops | bytes accessed | tf_op | source)
XLA Modules:
  0.0 61.5 jit_solution(3722237753183938050)
XLA Ops:
  0.6 1.0 %copy.9 = bf16[2,125,512]{2,1,0:T(8,128)(2,1)S(1)} copy(bf16[2,125,512]{2,0,1:T(2,128)(2,1)} %bitcast.17) | data formatting | bytes 512000
  1.6 0.0 copy-start
  1.6 1.1 %copy-done = bf16[256,3,512]{2,0,1:T(8,128)(2,1)S(1)} copy-done((bf16[256,3,512]{2,0,1:T(8,128)(2,1)S(1)}, bf16[256,3,512]{2,0,1:T(8,128)(2,1)}, u32[]{:S(2)}) %copy-start) | copy-done | bytes 786456
  2.8 0.0 copy-start.1
  2.8 0.7 %copy-done.1 = s32[256,1]{0,1:T(1,128)S(1)} copy-done((s32[256,1]{0,1:T(1,128)S(1)}, s32[256,1]{0,1:T(1,128)}, u32[]{:S(2)}) %copy-start.1) | copy-done | bytes 1048
  3.5 0.0 copy-start.2
  3.5 0.7 %copy-done.2 = s32[256]{0:T(256)S(1)} copy-done((s32[256]{0:T(256)S(1)}, s32[256]{0:T(256)}, u32[]{:S(2)}) %copy-start.2) | copy-done | bytes 1048
  4.1 0.0 copy-start.3
  4.1 0.7 %copy-done.3 = s32[256]{0:T(256)S(1)} copy-done((s32[256]{0:T(256)S(1)}, s32[256]{0:T(256)}, u32[]{:S(2)}) %copy-start.3) | copy-done | bytes 1048
  4.8 51.9 %shard_map.77 = (f32[5,5,5,5,8,128]{5,4,3,2,1,0:T(8,128)}, f32[3000,128]{1,0:T(8,128)S(1)}) custom-call(f32[5,5,5,5,8,128]{5,4,3,2,1,0:T(8,128)} %bitcast.16, bf16[3,256,512]{2,1,0:T(8,128)(2,1)S(1)} %bitcast.11, bf16[256,512]{1,0:T(8,128)(2,1)S(1)} %bitcast.10, s32[1,256]{1,0:T(1,128)S(1)} %bitcast.12, s32[1,256]{1,0:T(1,128)S(1)} %bitcast.13, ...), custom_call_target="tpu_custom_call" | custom-call | tf_op jit(solution)/shard_map/pallas_call | solution.py:495
  56.7 3.6 %copy.12 = f32[5,125,2,4,128]{4,3,2,1,0:T(4,128)} copy(f32[5,125,2,4,128]{4,3,2,1,0:T(4,128)} %bitcast.15) | data formatting | bytes 5120000
  60.3 1.1 %copy.13 = f32[3,125,2,4,128]{4,3,2,1,0:T(4,128)} copy(f32[3,125,2,4,128]{4,3,2,1,0:T(4,128)S(1)} %bitcast.9) | data formatting | bytes 3072000
  (1 shorter events, 0.0 us)
Async XLA Ops:
  1.6 1.1 %copy-start = (bf16[256,3,512]{2,0,1:T(8,128)(2,1)S(1)}, bf16[256,3,512]{2,0,1:T(8,128)(2,1)}, u32[]{:S(2)}) copy-start(bf16[256,3,512]{2,0,1:T(8,128)(2,1)} %param.6) | copy-start | bytes 2359300
  2.8 0.7 %copy-start.1 = (s32[256,1]{0,1:T(1,128)S(1)}, s32[256,1]{0,1:T(1,128)}, u32[]{:S(2)}) copy-start(s32[256,1]{0,1:T(1,128)} %param.7) | copy-start | bytes 3076
  3.5 0.7 %copy-start.2 = (s32[256]{0:T(256)S(1)}, s32[256]{0:T(256)}, u32[]{:S(2)}) copy-start(s32[256]{0:T(256)} %param.8) | copy-start | bytes 3076
  4.1 0.7 %copy-start.3 = (s32[256]{0:T(256)S(1)}, s32[256]{0:T(256)}, u32[]{:S(2)}) copy-start(s32[256]{0:T(256)} %param.9) | copy-start | bytes 3076
where the time goes:
time: 62.2 us; the launch traced here: 61.5 us
  Pallas kernels  51.9 us (83%)
  local copies, waits for them, and re-layouts  8.92 us (14%)
  between operations  0.66 us (1%)
    pallas_call x1, Pallas kernels, body(): pl.pallas_call(functools.partial(kernel, nax, naz), out_shape=(jax.ShapeD...  51.9 us
    unnamed x11, local copies, waits for them, and re-layouts  8.9 us

commit v1 on v0

v1 whole, which is shorter than its diff:
```python
import functools
import math

import jax
import jax.numpy as jnp
import numpy as np
from jax import lax
from jax.experimental import pallas as pl
from jax.experimental.pallas import tpu as pltpu
from jax.sharding import PartitionSpec as P

MACH = 0.3
SPEED = 1.3
DT = 0.03
LIFT = 10.0
VOLUME = 2.0
MAIL = 9
GROUP = 16
MESH = pl.DeviceIdType.MESH
F32 = jnp.float32
BF16 = jnp.bfloat16


def line_matrix():
    points = [-1.0, -math.sqrt(3.0 / 7.0), 0.0, math.sqrt(3.0 / 7.0), 1.0]
    bary = [
        1.0 / math.prod(points[c] - points[o] for o in range(5) if o != c) for c in range(5)
    ]
    d = np.zeros((5, 5))
    for i in range(5):
        for j in range(5):
            if i != j:
                d[i, j] = bary[j] / bary[i] / (points[i] - points[j])
        d[i, i] = -np.sum(d[i])
    return -VOLUME * d


D = line_matrix()


def deriv(x):
    e0, e1, o0, o1 = x[0] + x[4], x[1] + x[3], x[0] - x[4], x[1] - x[3]
    y = [None] * 5
    for i in range(2):
        odd = float(0.5 * (D[i, 0] - D[i, 4])) * o0 + float(0.5 * (D[i, 1] - D[i, 3])) * o1
        even = (
            float(0.5 * (D[i, 0] + D[i, 4])) * e0
            + float(0.5 * (D[i, 1] + D[i, 3])) * e1
            + float(D[i, 2]) * x[2]
        )
        y[i], y[4 - i] = odd + even, odd - even
    y[2] = float(D[2, 0]) * o0 + float(D[2, 1]) * o1
    return y


def cross_terms(jump, normal, along):
    t = (LIFT * normal) * jump[along]
    out = [None] * 5
    for f in (0, 4):
        out[f] = t - (LIFT * SPEED) * jump[f]
    for f in (1, 2, 3):
        out[f] = (-LIFT * SPEED) * jump[f]
    g = MACH * jump[1] + jump[0]
    out[along] = out[along] + (LIFT * normal) * g
    return out


def axial_terms(jump, normal):
    p, u, v, w, d = jump
    near = LIFT * (normal * MACH - SPEED)
    t = (LIFT * normal) * u
    return [
        near * p + t,
        near * u + (LIFT * normal) * p,
        (-LIFT * SPEED) * v,
        (-LIFT * SPEED) * w,
        near * d + t,
    ]


def unpack_faces(ref, index, tiles):
    parts = []
    for t in range(tiles):
        wide = ref[index + (slice(16 * t, 16 * t + 16), slice(None))].astype(F32)
        parts += [wide[:8], wide[8:]]
    return parts


def axial_lines(cur, nxt, left, right, b, r, low_half, emit):
    x = [[cur[f, a, b, r] for a in range(5)] for f in range(5)]
    p, u, d = x[0], x[1], x[4]
    diff = {
        0: deriv([MACH * p[a] + u[a] for a in range(5)]),
        1: deriv([MACH * u[a] + p[a] for a in range(5)]),
        4: deriv([MACH * d[a] + u[a] for a in range(5)]),
    }
    jump_lo, jump_hi = [], []
    for f in range(5):
        q = 5 * r + f
        m = q // 2
        if q % 2 == 0:
            halo = jnp.where(low_half, left[m], right[m])
        else:
            halo = pltpu.roll(jnp.where(low_half, right[m], left[m]), 4, 0)
        own = pltpu.roll(jnp.where(low_half, x[f][4], x[f][0]), 4, 0)
        jump_lo.append(x[f][0] - jnp.where(low_half, halo, own))
        jump_hi.append(x[f][4] - jnp.where(low_half, own, halo))
    lo, hi = axial_terms(jump_lo, -1.0), axial_terms(jump_hi, 1.0)
    for a in range(5):
        for f in range(5):
            total = nxt[f, a, b, r]
            if f in diff:
                total = total + diff[f][a]
            if a in (0, 4):
                total = total + (lo[f] if a == 0 else hi[f])
            emit(f, a, total)


def kernel(
    nax, naz,
    state_hbm, lamb_hbm, owner_hbm, element_hbm, class_hbm, table_ref,
    bufs, acc, s_ref, xl, xr,
    q_ref, lamb_ref, owner_ref, element_ref, class_ref, s_acc, post, inbox,
    xs, ys, yl, yr,
    load_sem, mail_send, mail_recv, xsend, xrecv, ysend, yrecv,
):
    n = nax * naz
    groups = n // GROUP
    ax, az = lax.axis_index("ax"), lax.axis_index("az")
    me = ax * naz + az
    has_left, has_right = ax > 0, ax < nax - 1
    az_up, az_down = lax.rem(az + 1, naz), lax.rem(az + naz - 1, naz)
    row = lax.broadcasted_iota(jnp.int32, (8, 128), 0)
    lane = lax.broadcasted_iota(jnp.int32, (8, 128), 1)
    low_half = row < 4
    ey = row & 3

    loads = [
        pltpu.make_async_copy(src, dst, load_sem.at[i])
        for i, (src, dst) in enumerate(
            [(owner_hbm, owner_ref), (element_hbm, element_ref), (class_hbm, class_ref),
             (lamb_hbm, lamb_ref), (state_hbm, q_ref)]
        )
    ]
    for load in loads:
        load.start()

    barrier = pltpu.get_barrier_semaphore()

    def greet(i, carry):
        other = lax.rem(me + i, n)
        pl.semaphore_signal(
            barrier, inc=1, device_id=(other // naz, lax.rem(other, naz)), device_id_type=MESH
        )
        return carry

    lax.fori_loop(1, n, greet, 0)

    @pl.when(jnp.logical_not(has_left))
    def _():
        def body(i, carry):
            for k in range(4):
                xl[k, i] = jnp.zeros(xl.shape[2:], BF16)
            return carry
        lax.fori_loop(0, 5, body, 0)

    @pl.when(jnp.logical_not(has_right))
    def _():
        def body(i, carry):
            for k in range(4):
                xr[k, i] = jnp.zeros(xr.shape[2:], BF16)
            return carry
        lax.fori_loop(0, 5, body, 0)

    for load in loads[:4]:
        load.wait()
    owner, element, shape_class = owner_ref[...], element_ref[...], class_ref[...]
    count = owner.shape[1]
    hit = lax.broadcasted_iota(jnp.int32, (n, count), 0) == owner
    hit = jnp.where(hit, 1.0, 0.0)
    earlier = lax.broadcasted_iota(jnp.int32, (count, count), 0) < lax.broadcasted_iota(
        jnp.int32, (count, count), 1
    )
    ranks = jnp.dot(
        hit.astype(BF16), jnp.where(earlier, 1.0, 0.0).astype(BF16), preferred_element_type=F32
    )
    position = jnp.sum(hit * ranks, axis=0, keepdims=True).astype(jnp.int32)
    values, largest = [], None
    for c in range(3):
        both = lax.dot_general(
            table_ref[...], lamb_ref[c], (((1,), (1,)), ((), ())), preferred_element_type=F32
        )
        value = jnp.where(shape_class == 0, both[:128], both[128:])
        values.append(value)
        top = jnp.max(jnp.abs(value), axis=0, keepdims=True)
        largest = top if largest is None else jnp.maximum(largest, top)
    shift = 14.0 - jnp.floor(jnp.log2(jnp.maximum(largest, 1e-30)))
    gain = jnp.exp2(shift)
    node_row = lax.broadcasted_iota(jnp.int32, (128, count), 0)
    digits = []
    for c in range(3):
        fixed = jnp.clip(jnp.floor(values[c] * gain + 0.5), -32767.0, 32767.0)
        if c == 0:
            fixed = jnp.where(node_row == 125, (element + 1).astype(F32), fixed)
        if c == 1:
            fixed = jnp.where(node_row == 125, shift, fixed)
        high = jnp.floor((fixed + 128.0) * (1.0 / 256.0))
        digits.append([high.astype(BF16), (fixed - 256.0 * high).astype(BF16)])
    slot_row = lax.broadcasted_iota(jnp.int32, (n * 8, count), 0)

    def placed(slot, fields):
        place = jnp.where(slot_row == slot, 1.0, 0.0).astype(BF16)
        out = []
        for c in fields:
            mail = lax.dot_general(
                place, jnp.concatenate(digits[c], axis=0), (((1,), (1,)), ((), ())),
                preferred_element_type=F32,
            )
            out.append((256.0 * mail[:, :128] + mail[:, 128:]).astype(jnp.int32))
        return out

    early = position < 3
    first, second = placed(owner * 8 + position, (0, 1))
    (upper,) = placed(jnp.where(early, owner * 8 + ((position + 6) & 7), -1), (2,))
    (lower,) = placed(jnp.where(early, -1, owner * 8 + ((position + 3) & 7)), (2,))
    pair = ((first << 16) + second).reshape(n, 8, 128)
    third = ((upper << 16) + lower).reshape(n, 8, 128)
    tile_row = lax.broadcasted_iota(jnp.int32, (n, 8, 128), 1)
    post[:, 0:8] = jnp.where(tile_row < 6, pair, third)
    post[:, 8:16] = third

    def x_copy(k, b, side):
        if side == 0:
            dst, dev = xl, (ax + 1, az)
        else:
            dst, dev = xr, (ax - 1, az)
        return pltpu.make_async_remote_copy(
            src_ref=xs.at[k, b, side], dst_ref=dst.at[k, b], send_sem=xsend.at[k, b, side],
            recv_sem=xrecv.at[k, b, side], device_id=dev, device_id_type=MESH,
        )

    def y_copy(k, side):
        if side == 0:
            dst, dev = yl, (ax, az_up)
        else:
            dst, dev = yr, (ax, az_down)
        return pltpu.make_async_remote_copy(
            src_ref=ys.at[k, side], dst_ref=dst.at[k], send_sem=ysend.at[k, side],
            recv_sem=yrecv.at[k, side], device_id=dev, device_id_type=MESH,
        )

    def pack_x(ref, k, b):
        for side in range(2):
            a = 4 if side == 0 else 0
            parts = []
            for m in range(14):
                pair = []
                for q in (2 * m, 2 * m + 1):
                    pair.append(ref[q % 5, a, b, q // 5] if q < 25 else jnp.zeros((8, 128), F32))
                even, odd = pltpu.roll(pair[0], 4, 0), pair[1]
                parts.append(
                    jnp.where(low_half, even, odd) if side == 0 else jnp.where(low_half, odd, even)
                )
            for t in range(7):
                xs[k, b, side, 16 * t:16 * t + 16, :] = jnp.concatenate(
                    [parts[2 * t], parts[2 * t + 1]], axis=0
                ).astype(BF16)

    def pack_y(ref, k, side):
        b = 4 if side == 0 else 0

        def body(a, carry):
            parts = []
            for m in range(8):
                total = jnp.zeros((8, 128), F32)
                for j in range(4):
                    q = 4 * m + j
                    if q < 25:
                        turn = (j - 3) % 8 if side == 0 else (3 + j) % 8
                        value = ref[q % 5, a, b, q // 5]
                        value = pltpu.roll(value, turn, 0) if turn else value
                        residue = j if side == 0 else (3 + j) % 4
                        total = jnp.where(ey == residue, value, total)
                parts.append(total)
            for t in range(4):
                ys[k, side, a, 16 * t:16 * t + 16, :] = jnp.concatenate(
                    [parts[2 * t], parts[2 * t + 1]], axis=0
                ).astype(BF16)
            return carry

        lax.fori_loop(0, 5, body, 0)

    def send_x(k, b):
        @pl.when(has_right)
        def _():
            x_copy(k, b, 0).start()

        @pl.when(has_left)
        def _():
            x_copy(k, b, 1).start()

    def take_x(k, b):
        @pl.when(has_left)
        def _():
            x_copy(k, b, 0).wait_recv()

        @pl.when(has_right)
        def _():
            x_copy(k, b, 1).wait_recv()

    pl.semaphore_wait(barrier, n - 1)

    def mail_out(i, carry):
        other = lax.rem(me + i, n)
        pltpu.make_async_remote_copy(
            src_ref=post.at[other, pl.ds(0, MAIL)], dst_ref=inbox.at[i, pl.ds(0, MAIL)],
            send_sem=mail_send, recv_sem=mail_recv.at[i // GROUP],
            device_id=(other // naz, lax.rem(other, naz)), device_id_type=MESH,
        ).start()
        return carry

    lax.fori_loop(1, n, mail_out, 0)
    inbox[0] = post[me]

    loads[4].wait()
    pack_y(q_ref, 0, 0)
    y_copy(0, 0).start()
    pack_y(q_ref, 0, 1)
    y_copy(0, 1).start()

    def first_x(b, carry):
        pack_x(q_ref, 0, b)
        send_x(0, b)
        return carry

    lax.fori_loop(0, 5, first_x, 0)

    def z_pass(cur, nxt):
        def body(a, carry):
            for b in range(5):
                x = [[cur[f, a, b, r] for r in range(5)] for f in range(5)]
                dw = deriv(x[3])
                dg = deriv([MACH * x[1][r] + x[0][r] for r in range(5)])
                lo = cross_terms(
                    [x[f][0] - jnp.where(lane == 0, 0.0, pltpu.roll(x[f][4], 1, 1)) for f in range(5)],
                    -1.0, 3,
                )
                hi = cross_terms(
                    [x[f][4] - jnp.where(lane == 127, 0.0, pltpu.roll(x[f][0], 127, 1)) for f in range(5)],
                    1.0, 3,
                )
                for r in range(5):
                    for f in range(5):
                        value = dw[r] if f in (0, 4) else dg[r] if f == 3 else None
                        face = lo[f] if r == 0 else hi[f] if r == 4 else None
                        if value is None:
                            value = jnp.zeros((8, 128), F32) if face is None else face
                        elif face is not None:
                            value = value + face
                        nxt[f, a, b, r] = value
            return carry

        lax.fori_loop(0, 5, body, 0)

    def y_pass(cur, nxt, k):
        y_copy(k, 0).wait_recv()
        y_copy(k, 1).wait_recv()

        def body(a, carry):
            down, up = unpack_faces(yl, (k, a), 4), unpack_faces(yr, (k, a), 4)
            for r in range(5):
                x = [[cur[f, a, b, r] for b in range(5)] for f in range(5)]
                dv = deriv(x[2])
                dg = deriv([MACH * x[1][b] + x[0][b] for b in range(5)])
                jump_lo, jump_hi = [], []
                for f in range(5):
                    q = 5 * r + f
                    j = q % 4
                    halo = jnp.where(ey == j, down[q // 4], up[q // 4])
                    halo = pltpu.roll(halo, 8 - j, 0) if j else halo
                    jump_lo.append(x[f][0] - jnp.where(ey == 0, halo, pltpu.roll(x[f][4], 1, 0)))
                    jump_hi.append(x[f][4] - jnp.where(ey == 3, halo, pltpu.roll(x[f][0], 7, 0)))
                lo, hi = cross_terms(jump_lo, -1.0, 2), cross_terms(jump_hi, 1.0, 2)
                for b in range(5):
                    for f in range(5):
                        value = dv[b] if f in (0, 4) else dg[b] if f == 2 else None
                        face = lo[f] if b == 0 else hi[f] if b == 4 else None
                        if value is None and face is None:
                            continue
                        if value is None:
                            value = face
                        elif face is not None:
                            value = value + face
                        nxt[f, a, b, r] = nxt[f, a, b, r] + value
            return carry

        lax.fori_loop(0, 5, body, 0)

    def x_pass(cur, nxt, k, scale, first):
        def body(i, carry):
            b = jnp.where(i == 0, 0, jnp.where(i == 1, 4, i - 1))
            take_x(k, b)
            left, right = unpack_faces(xl, (k, b), 7), unpack_faces(xr, (k, b), 7)
            for r in range(5):
                def emit(f, a, total):
                    if first and f in (1, 2, 3):
                        at = ((f - 1) * 125 + a * 25 + b * 5 + r) * 8
                        total = total + s_ref[pl.ds(pl.multiple_of(at, 8), 8), :]
                    total = scale * total
                    nxt[f, a, b, r] = total
                    before = q_ref[f, a, b, r] if first else acc[f, a, b, r]
                    acc[f, a, b, r] = before + total

                axial_lines(cur, nxt, left, right, b, r, low_half, emit)

            pack_x(nxt, k + 1, b)
            send_x(k + 1, b)

            @pl.when(i == 0)
            def _():
                pack_y(nxt, k + 1, 1)
                y_copy(k + 1, 1).start()

            @pl.when(i == 1)
            def _():
                pack_y(nxt, k + 1, 0)
                y_copy(k + 1, 0).start()
            return carry

        lax.fori_loop(0, 5, body, 0)

    z_pass(q_ref, bufs.at[0])
    y_pass(q_ref, bufs.at[0], 0)

    def mail_block(first_one, many, g):
        return pltpu.make_async_remote_copy(
            src_ref=post.at[pl.ds(first_one, many), pl.ds(0, MAIL)],
            dst_ref=inbox.at[pl.ds(first_one, many), pl.ds(0, MAIL)],
            send_sem=mail_send, recv_sem=mail_recv.at[g],
            device_id=(ax, az), device_id_type=MESH,
        )

    def opened(g):
        block = inbox[pl.ds(g * GROUP, GROUP)]
        upper, lower = block[:, 0:8], block[:, 8:16]
        at = lax.broadcasted_iota(jnp.int32, (GROUP, 8, 128), 1)
        second = (upper << 16) >> 16
        first = (upper - second) >> 16
        third = jnp.where(at >= 6, upper, lower)
        early, late = pltpu.roll(third, 2, 1), pltpu.roll(third, 5, 1)
        third = jnp.where(at < 3, (early - ((early << 16) >> 16)) >> 16, (late << 16) >> 16)
        rows = [
            jnp.where(at < 6, x, 0).astype(F32).reshape(GROUP * 8, 128)
            for x in (first, second, third)
        ]
        code = rows[0][:, 125:126].astype(jnp.int32) - 1
        scale = jnp.exp2(-rows[1][:, 125:126])
        turned = jnp.concatenate([(x * scale).T for x in rows], axis=0)
        high = turned.astype(BF16)
        low = (turned - high.astype(F32)).astype(BF16)
        return code, jnp.concatenate([high, low], axis=1)

    def sums(code, lines, t):
        member = code == lax.broadcasted_iota(jnp.int32, (GROUP * 8, 256), 1) + 256 * t
        member = jnp.where(member, 1.0, 0.0).astype(BF16)
        return jnp.dot(
            lines, jnp.concatenate([member, member], axis=0), preferred_element_type=F32
        )

    def gather_first():
        mail_block(1, GROUP - 1, 0).wait_recv()
        code, lines = opened(0)
        for t in range(4):
            s_acc[:, 256 * t:256 * t + 256] = sums(code, lines, t)

    def gather(g, carry):
        mail_block(g * GROUP, GROUP, g).wait_recv()
        code, lines = opened(g)
        for t in range(4):
            s_acc[:, 256 * t:256 * t + 256] += sums(code, lines, t)
        return carry

    def gather_last():
        mail_block((groups - 1) * GROUP, GROUP, groups - 1).wait_recv()
        code, lines = opened(groups - 1)
        for t in range(4):
            total = s_acc[:, 256 * t:256 * t + 256] + sums(code, lines, t)
            for c in range(3):
                for h in range(2):
                    s_ref[pl.ds(c * 1000 + 2 * t + h, 125, stride=8), :] = total[
                        128 * c:128 * c + 125, 128 * h:128 * h + 128
                    ]

    gather_first()
    lax.fori_loop(1, groups - 1, gather, 0)
    gather_last()

    x_pass(q_ref, bufs.at[0], 0, DT, True)

    def stage(k, carry):
        cur, nxt = bufs.at[lax.rem(k + 1, 2)], bufs.at[lax.rem(k, 2)]
        scale = jnp.where(k == 1, DT / 2.0, DT / 3.0)
        z_pass(cur, nxt)
        y_pass(cur, nxt, k)
        x_pass(cur, nxt, k, scale, False)
        return carry

    lax.fori_loop(1, 3, stage, 0)
    z_pass(bufs.at[0], bufs.at[1])
    y_pass(bufs.at[0], bufs.at[1], 3)

    mail_block(0, n - 1, 0).wait_send()

    def drain(k, carry):
        y_copy(k, 0).wait_send()
        y_copy(k, 1).wait_send()

        def inner(b, carry):
            @pl.when(has_right)
            def _():
                x_copy(k, b, 0).wait_send()

            @pl.when(has_left)
            def _():
                x_copy(k, b, 1).wait_send()
            return carry

        lax.fori_loop(0, 5, inner, 0)
        return carry

    lax.fori_loop(0, 4, drain, 0)
    for b in range(5):
        take_x(3, b)


def finish(bufs, acc, s_ref, xl, xr, new_hbm, source_hbm, new_ref, sem):
    save_source = pltpu.make_async_copy(s_ref, source_hbm, sem.at[5])
    save_source.start()
    low_half = lax.broadcasted_iota(jnp.int32, (8, 128), 0) < 4
    cur, nxt = bufs.at[0], bufs.at[1]

    def save(b):
        return pltpu.make_async_copy(new_ref.at[:, :, b], new_hbm.at[:, :, b], sem.at[b])

    def body(b, carry):
        left, right = unpack_faces(xl, (3, b), 7), unpack_faces(xr, (3, b), 7)
        for r in range(5):
            def emit(f, a, total):
                new_ref[f, a, b, r] = acc[f, a, b, r] + (DT / 4.0) * total

            axial_lines(cur, nxt, left, right, b, r, low_half, emit)
        save(b).start()
        return carry

    lax.fori_loop(0, 5, body, 0)
    for b in range(5):
        save(b).wait()
    save_source.wait()


def body(nax, naz, lamb_vector, owner, element, shape_class, interp_tables, acoustic_state):
    n = nax * naz
    count = lamb_vector.shape[0]
    lamb = jnp.transpose(lamb_vector, (1, 0, 2))
    table = jnp.pad(jnp.transpose(interp_tables, (0, 2, 1)), ((0, 0), (0, 3), (0, 0)))
    table = table.reshape(256, 512)
    nodes = (5, 5, 5, 5, 8, 128)
    state = acoustic_state.reshape(nodes)
    vmem, hbm = pl.BlockSpec(memory_space=pltpu.VMEM), pl.BlockSpec(memory_space=pltpu.HBM)
    dma = pltpu.SemaphoreType.DMA
    kept = pl.pallas_call(
        functools.partial(kernel, nax, naz),
        out_shape=(
            jax.ShapeDtypeStruct((2,) + nodes, F32),
            jax.ShapeDtypeStruct(nodes, F32),
            jax.ShapeDtypeStruct((3000, 128), F32),
            jax.ShapeDtypeStruct((4, 5, 112, 128), BF16),
            jax.ShapeDtypeStruct((4, 5, 112, 128), BF16),
        ),
        in_specs=[hbm] * 5 + [vmem],
        out_specs=(vmem,) * 5,
        scratch_shapes=[
            pltpu.VMEM(nodes, F32),
            pltpu.VMEM(lamb.shape, BF16),
            pltpu.VMEM((1, count), jnp.int32),
            pltpu.VMEM((1, count), jnp.int32),
            pltpu.VMEM((1, count), jnp.int32),
            pltpu.VMEM((384, 1024), F32),
            pltpu.VMEM((n, 16, 128), jnp.int32),
            pltpu.VMEM((n, 16, 128), jnp.int32),
            pltpu.VMEM((4, 5, 2, 112, 128), BF16),
            pltpu.VMEM((4, 2, 5, 64, 128), BF16),
            pltpu.VMEM((4, 5, 64, 128), BF16),
            pltpu.VMEM((4, 5, 64, 128), BF16),
            dma((5,)), dma, dma((n // GROUP,)),
            dma((4, 5, 2)), dma((4, 5, 2)), dma((4, 2)), dma((4, 2)),
        ],
        compiler_params=pltpu.CompilerParams(
            collective_id=0, has_side_effects=True, vmem_limit_bytes=36 * 1024 * 1024
        ),
    )(
        state, lamb,
        owner.reshape(1, count), element.reshape(1, count), shape_class.reshape(1, count), table,
    )
    new, source = pl.pallas_call(
        finish,
        out_shape=(jax.ShapeDtypeStruct(nodes, F32), jax.ShapeDtypeStruct((3000, 128), F32)),
        in_specs=[vmem] * 5,
        out_specs=(hbm, hbm),
        scratch_shapes=[pltpu.VMEM(nodes, F32), dma((6,))],
        compiler_params=pltpu.CompilerParams(vmem_limit_bytes=24 * 1024 * 1024),
    )(*kept)
    return new.reshape(5, 125, 2, 4, 128), source.reshape(3, 125, 2, 4, 128)


def solution(mesh):
    nax, naz = mesh.shape["ax"], mesh.shape["az"]
    in_specs = (
        P(("ax", "az"), None, None),
        P(("ax", "az"), None),
        P(("ax", "az")),
        P(("ax", "az")),
        P(),
        P(None, None, "ax", "az", None),
    )
    out_specs = (P(None, None, "ax", "az", None), P(None, None, "ax", "az", None))
    return jax.shard_map(
        functools.partial(body, nax, naz), mesh=mesh, in_specs=in_specs, out_specs=out_specs,
        check_vma=False,
    )
```

time: 62.2 us -> 49 us (0.79)
  Pallas kernels: 51.9 us -> 41.7 us
  local copies, waits for them, and re-layouts: 8.92 us -> 5.88 us
    pallas_call x1, Pallas kernels: 51.9 us -> 39.7 us  [body(): pl.pallas_call(functools.partial(kernel, nax, naz), out_shape=(jax.ShapeD...]
    unnamed x11, local copies, waits for them, and re-layouts: 8.9 us -> 5.86 us
    pallas_call x0 -> x1, Pallas kernels: none -> 2.02 us  [body(): pl.pallas_call(finish, out_shape=(jax.ShapeDtypeStruct(nodes, F32), jax.S...]
where the time goes in v1:
time: 49 us; the launch traced here: 48.3 us
  Pallas kernels  41.7 us (85%)
  local copies, waits for them, and re-layouts  5.88 us (12%)
  between operations  0.66 us (1%)
    pallas_call x1, Pallas kernels, body(): pl.pallas_call(functools.partial(kernel, nax, naz), out_shape=(jax.ShapeD...  39.7 us
    unnamed x11, local copies, waits for them, and re-layouts  5.86 us
    pallas_call x1, Pallas kernels, body(): pl.pallas_call(finish, out_shape=(jax.ShapeDtypeStruct(nodes, F32), jax.S...  2.02 us

profile of v1, /device:TPU:32, one launch (start us, length us, event | category | flops | bytes accessed | tf_op | source)
XLA Modules:
  0.0 48.3 jit_solution(1143644199487392707)
XLA Ops:
  0.6 1.0 %copy.9 = bf16[2,125,512]{2,1,0:T(8,128)(2,1)S(1)} copy(bf16[2,125,512]{2,0,1:T(2,128)(2,1)} %bitcast.15) | data formatting | bytes 512000
  1.6 0.0 copy-start
  1.6 1.7 %copy-done = f32[5,125,2,4,128]{4,3,2,1,0:T(4,128)S(1)} copy-done((f32[5,125,2,4,128]{4,3,2,1,0:T(4,128)S(1)}, f32[5,125,2,4,128]{4,3,2,1,0:T(4,128)}, u32[]{:S(2)}) %copy-start) | copy-done | bytes 2560024
  3.4 0.0 copy-start.1
  3.4 1.1 %copy-done.1 = bf16[256,3,512]{2,0,1:T(8,128)(2,1)S(1)} copy-done((bf16[256,3,512]{2,0,1:T(8,128)(2,1)S(1)}, bf16[256,3,512]{2,0,1:T(8,128)(2,1)}, u32[]{:S(2)}) %copy-start.1) | copy-done | bytes 786456
  4.5 0.0 copy-start.2
  4.5 0.7 %copy-done.2 = s32[256,1]{0,1:T(1,128)S(1)} copy-done((s32[256,1]{0,1:T(1,128)S(1)}, s32[256,1]{0,1:T(1,128)}, u32[]{:S(2)}) %copy-start.2) | copy-done | bytes 1048
  5.2 0.0 copy-start.3
  5.2 0.7 %copy-done.3 = s32[256]{0:T(256)S(1)} copy-done((s32[256]{0:T(256)S(1)}, s32[256]{0:T(256)}, u32[]{:S(2)}) %copy-start.3) | copy-done | bytes 1048
  5.9 0.0 copy-start.4
  5.9 0.7 %copy-done.4 = s32[256]{0:T(256)S(1)} copy-done((s32[256]{0:T(256)S(1)}, s32[256]{0:T(256)}, u32[]{:S(2)}) %copy-start.4) | copy-done | bytes 1048
  6.5 39.7 %shard_map.77 = (f32[2,5,5,5,5,8,128]{6,5,4,3,2,1,0:T(8,128)S(1)}, f32[5,5,5,5,8,128]{5,4,3,2,1,0:T(8,128)S(1)}, f32[3000,128]{1,0:T(8,128)S(1)}, bf16[4,5,112,1...) custom-call(f32[5,5,5,5,8,128]{5,4,3,2,1,0:T(8,128)S(1)} %bitcast.9, bf16[3,256,512]{2,1,0:T(8,128)(2,1)S(1)} %bitcast.11, ...), custom_call_target="tpu_custom_call" | custom-call | tf_op jit(solution)/shard_map/pallas_call | solution.py:571
  46.3 2.0 %shard_map.78 = (f32[5,5,5,5,8,128]{5,4,3,2,1,0:T(8,128)}, f32[3000,128]{1,0:T(8,128)}) custom-call(f32[2,5,5,5,5,8,128]{6,5,4,3,2,1,0:T(8,128)S(1)} %get-tuple-element.9.bufs, f32[5,5,5,5,8,128]{5,4,3,2,1,0:T(8,128)S(1)} %get-tuple-element.10.acc, f32[3000,128]{1,0:T(8,128)S(1)} %get-tuple-element.11.s_ref, ...), custom_call_target="tpu_custom_call" | custom-call | tf_op jit(solution)/shard_map/pallas_call | solution.py:605
  (1 shorter events, 0.0 us)
Async XLA Ops:
  1.6 1.7 %copy-start = (f32[5,125,2,4,128]{4,3,2,1,0:T(4,128)S(1)}, f32[5,125,2,4,128]{4,3,2,1,0:T(4,128)}, u32[]{:S(2)}) copy-start(f32[5,125,2,4,128]{4,3,2,1,0:T(4,128)} %param.11) | copy-start | bytes 7680004
  3.4 1.1 %copy-start.1 = (bf16[256,3,512]{2,0,1:T(8,128)(2,1)S(1)}, bf16[256,3,512]{2,0,1:T(8,128)(2,1)}, u32[]{:S(2)}) copy-start(bf16[256,3,512]{2,0,1:T(8,128)(2,1)} %param.6) | copy-start | bytes 2359300
  4.5 0.7 %copy-start.2 = (s32[256,1]{0,1:T(1,128)S(1)}, s32[256,1]{0,1:T(1,128)}, u32[]{:S(2)}) copy-start(s32[256,1]{0,1:T(1,128)} %param.7) | copy-start | bytes 3076
  5.2 0.7 %copy-start.3 = (s32[256]{0:T(256)S(1)}, s32[256]{0:T(256)}, u32[]{:S(2)}) copy-start(s32[256]{0:T(256)} %param.8) | copy-start | bytes 3076
  5.9 0.7 %copy-start.4 = (s32[256]{0:T(256)S(1)}, s32[256]{0:T(256)}, u32[]{:S(2)}) copy-start(s32[256]{0:T(256)} %param.9) | copy-start | bytes 3076

commit v2 on v1

--- a/solution.py
+++ b/solution.py
@@ -118,9 +118,9 @@
 
 def kernel(
     nax, naz,
-    state_hbm, lamb_hbm, owner_hbm, element_hbm, class_hbm, table_ref,
-    bufs, acc, s_ref, xl, xr,
-    q_ref, lamb_ref, owner_ref, element_ref, class_ref, s_acc, post, inbox,
+    state_hbm, lamb_hbm, key_ref, table_ref,
+    even, odd, acc, s_ref, xl, xr,
+    lamb_ref, s_acc, post, inbox,
     xs, ys, yl, yr,
     load_sem, mail_send, mail_recv, xsend, xrecv, ysend, yrecv,
 ):
@@ -138,8 +138,7 @@
     loads = [
         pltpu.make_async_copy(src, dst, load_sem.at[i])
         for i, (src, dst) in enumerate(
-            [(owner_hbm, owner_ref), (element_hbm, element_ref), (class_hbm, class_ref),
-             (lamb_hbm, lamb_ref), (state_hbm, q_ref)]
+            [(lamb_hbm, lamb_ref), (state_hbm, even), (state_hbm, acc)]
         )
     ]
     for load in loads:
@@ -172,9 +171,8 @@
             return carry
         lax.fori_loop(0, 5, body, 0)
 
-    for load in loads[:4]:
-        load.wait()
-    owner, element, shape_class = owner_ref[...], element_ref[...], class_ref[...]
+    key = key_ref[...]
+    owner, element, shape_class = lax.rem(key, n), (key // n) >> 1, (key // n) & 1
     count = owner.shape[1]
     hit = lax.broadcasted_iota(jnp.int32, (n, count), 0) == owner
     hit = jnp.where(hit, 1.0, 0.0)
@@ -186,6 +184,7 @@
     )
     position = jnp.sum(hit * ranks, axis=0, keepdims=True).astype(jnp.int32)
     values, largest = [], None
+    loads[0].wait()
     for c in range(3):
         both = lax.dot_general(
             table_ref[...], lamb_ref[c], (((1,), (1,)), ((), ())), preferred_element_type=F32
@@ -322,18 +321,19 @@
     lax.fori_loop(1, n, mail_out, 0)
     inbox[0] = post[me]
 
-    loads[4].wait()
-    pack_y(q_ref, 0, 0)
+    loads[1].wait()
+    pack_y(even, 0, 0)
     y_copy(0, 0).start()
-    pack_y(q_ref, 0, 1)
+    pack_y(even, 0, 1)
     y_copy(0, 1).start()
 
     def first_x(b, carry):
-        pack_x(q_ref, 0, b)
+        pack_x(even, 0, b)
         send_x(0, b)
         return carry
 
     lax.fori_loop(0, 5, first_x, 0)
+    loads[2].wait()
 
     def z_pass(cur, nxt):
         def body(a, carry):
@@ -362,25 +362,18 @@
 
         lax.fori_loop(0, 5, body, 0)
 
-    def y_pass(cur, nxt, k):
-        y_copy(k, 0).wait_recv()
-        y_copy(k, 1).wait_recv()
-
+    def y_pass(cur, nxt):
         def body(a, carry):
-            down, up = unpack_faces(yl, (k, a), 4), unpack_faces(yr, (k, a), 4)
             for r in range(5):
                 x = [[cur[f, a, b, r] for b in range(5)] for f in range(5)]
                 dv = deriv(x[2])
                 dg = deriv([MACH * x[1][b] + x[0][b] for b in range(5)])
                 jump_lo, jump_hi = [], []
                 for f in range(5):
-                    q = 5 * r + f
-                    j = q % 4
-                    halo = jnp.where(ey == j, down[q // 4], up[q // 4])
-                    halo = pltpu.roll(halo, 8 - j, 0) if j else halo
-                    jump_lo.append(x[f][0] - jnp.where(ey == 0, halo, pltpu.roll(x[f][4], 1, 0)))
-                    jump_hi.append(x[f][4] - jnp.where(ey == 3, halo, pltpu.roll(x[f][0], 7, 0)))
+                    jump_lo.append(x[f][0] - jnp.where(ey == 0, 0.0, pltpu.roll(x[f][4], 1, 0)))
+                    jump_hi.append(x[f][4] - jnp.where(ey == 3, 0.0, pltpu.roll(x[f][0], 7, 0)))
                 lo, hi = cross_terms(jump_lo, -1.0, 2), cross_terms(jump_hi, 1.0, 2)
+                ready = []
                 for b in range(5):
                     for f in range(5):
                         value = dv[b] if f in (0, 4) else dg[b] if f == 2 else None
@@ -391,46 +384,70 @@
                             value = face
                         elif face is not None:
                             value = value + face
-                        nxt[f, a, b, r] = nxt[f, a, b, r] + value
-            return carry
-
-        lax.fori_loop(0, 5, body, 0)
-
-    def x_pass(cur, nxt, k, scale, first):
+                        ready.append((f, b, nxt[f, a, b, r] + value))
+                for f, b, value in ready:
+                    nxt[f, a, b, r] = value
+            return carry
+
+        lax.fori_loop(0, 5, body, 0)
+
+    def y_fix(nxt, k, side):
+        b, normal, edge = (0, -1.0, 0) if side == 0 else (4, 1.0, 3)
+        y_copy(k, side).wait_recv()
+
+        def body(a, carry):
+            faces = unpack_faces(yl if side == 0 else yr, (k, a), 4)
+            for r in range(5):
+                jump = []
+                for f in range(5):
+                    q = 5 * r + f
+                    j = q % 4
+                    halo = pltpu.roll(faces[q // 4], 8 - j, 0) if j else faces[q // 4]
+                    jump.append(jnp.where(ey == edge, -halo, 0.0))
+                ready = [nxt[f, a, b, r] + t for f, t in enumerate(cross_terms(jump, normal, 2))]
+                for f in range(5):
+                    nxt[f, a, b, r] = ready[f]
+            return carry
+
+        lax.fori_loop(0, 5, body, 0)
+
+    def x_pass(cur, nxt, k, scale):
         def body(i, carry):
-            b = jnp.where(i == 0, 0, jnp.where(i == 1, 4, i - 1))
+            b = jnp.where(i == 3, 0, jnp.where(i == 4, 4, i + 1))
+
+            @pl.when(i == 3)
+            def _():
+                y_fix(nxt, k, 0)
+
+            @pl.when(i == 4)
+            def _():
+                y_fix(nxt, k, 1)
+
             take_x(k, b)
             left, right = unpack_faces(xl, (k, b), 7), unpack_faces(xr, (k, b), 7)
             for r in range(5):
                 def emit(f, a, total):
-                    if first and f in (1, 2, 3):
-                        at = ((f - 1) * 125 + a * 25 + b * 5 + r) * 8
-                        total = total + s_ref[pl.ds(pl.multiple_of(at, 8), 8), :]
                     total = scale * total
                     nxt[f, a, b, r] = total
-                    before = q_ref[f, a, b, r] if first else acc[f, a, b, r]
-                    acc[f, a, b, r] = before + total
+                    acc[f, a, b, r] = acc[f, a, b, r] + total
 
                 axial_lines(cur, nxt, left, right, b, r, low_half, emit)
 
             pack_x(nxt, k + 1, b)
             send_x(k + 1, b)
 
-            @pl.when(i == 0)
+            @pl.when(i == 3)
             def _():
                 pack_y(nxt, k + 1, 1)
                 y_copy(k + 1, 1).start()
 
-            @pl.when(i == 1)
+            @pl.when(i == 4)
             def _():
                 pack_y(nxt, k + 1, 0)
                 y_copy(k + 1, 0).start()
             return carry
 
         lax.fori_loop(0, 5, body, 0)
-
-    z_pass(q_ref, bufs.at[0])
-    y_pass(q_ref, bufs.at[0], 0)
 
     def mail_block(first_one, many, g):
         return pltpu.make_async_remote_copy(
@@ -491,23 +508,30 @@
                         128 * c:128 * c + 125, 128 * h:128 * h + 128
                     ]
 
-    gather_first()
-    lax.fori_loop(1, groups - 1, gather, 0)
-    gather_last()
-
-    x_pass(q_ref, bufs.at[0], 0, DT, True)
-
-    def stage(k, carry):
-        cur, nxt = bufs.at[lax.rem(k + 1, 2)], bufs.at[lax.rem(k, 2)]
-        scale = jnp.where(k == 1, DT / 2.0, DT / 3.0)
+    def add_source(nxt):
+        def body(i, carry):
+            for j in range(25):
+                a, b, r = i, j // 5, j % 5
+                for c in range(3):
+                    at = (c * 125 + i * 25 + j) * 8
+                    nxt[c + 1, a, b, r] = (
+                        nxt[c + 1, a, b, r] + s_ref[pl.ds(pl.multiple_of(at, 8), 8), :]
+                    )
+            return carry
+
+        lax.fori_loop(0, 5, body, 0)
+
+    for k in range(4):
+        cur, nxt = (even, odd) if k % 2 == 0 else (odd, even)
         z_pass(cur, nxt)
-        y_pass(cur, nxt, k)
-        x_pass(cur, nxt, k, scale, False)
-        return carry
-
-    lax.fori_loop(1, 3, stage, 0)
-    z_pass(bufs.at[0], bufs.at[1])
-    y_pass(bufs.at[0], bufs.at[1], 3)
+        y_pass(cur, nxt)
+        if k == 0:
+            gather_first()
+            lax.fori_loop(1, groups - 1, gather, 0)
+            gather_last()
+            add_source(nxt)
+        if k < 3:
+            x_pass(cur, nxt, k, DT / (k + 1))
 
     mail_block(0, n - 1, 0).wait_send()
 
@@ -529,15 +553,16 @@
         return carry
 
     lax.fori_loop(0, 4, drain, 0)
+    y_fix(even, 3, 0)
+    y_fix(even, 3, 1)
     for b in range(5):
         take_x(3, b)
 
 
-def finish(bufs, acc, s_ref, xl, xr, new_hbm, source_hbm, new_ref, sem):
+def finish(nxt, cur, acc, s_ref, xl, xr, new_hbm, source_hbm, new_ref, sem):
     save_source = pltpu.make_async_copy(s_ref, source_hbm, sem.at[5])
     save_source.start()
     low_half = lax.broadcasted_iota(jnp.int32, (8, 128), 0) < 4
-    cur, nxt = bufs.at[0], bufs.at[1]
 
     def save(b):
         return pltpu.make_async_copy(new_ref.at[:, :, b], new_hbm.at[:, :, b], sem.at[b])
@@ -566,25 +591,23 @@
     table = table.reshape(256, 512)
     nodes = (5, 5, 5, 5, 8, 128)
     state = acoustic_state.reshape(nodes)
+    key = ((element * 2 + shape_class) * n + owner[:, 0]).reshape(1, count)
     vmem, hbm = pl.BlockSpec(memory_space=pltpu.VMEM), pl.BlockSpec(memory_space=pltpu.HBM)
     dma = pltpu.SemaphoreType.DMA
     kept = pl.pallas_call(
         functools.partial(kernel, nax, naz),
         out_shape=(
-            jax.ShapeDtypeStruct((2,) + nodes, F32),
+            jax.ShapeDtypeStruct(nodes, F32),
+            jax.ShapeDtypeStruct(nodes, F32),
             jax.ShapeDtypeStruct(nodes, F32),
             jax.ShapeDtypeStruct((3000, 128), F32),
             jax.ShapeDtypeStruct((4, 5, 112, 128), BF16),
             jax.ShapeDtypeStruct((4, 5, 112, 128), BF16),
         ),
-        in_specs=[hbm] * 5 + [vmem],
-        out_specs=(vmem,) * 5,
+        in_specs=[hbm, hbm, vmem, vmem],
+        out_specs=(vmem,) * 6,
         scratch_shapes=[
-            pltpu.VMEM(nodes, F32),
             pltpu.VMEM(lamb.shape, BF16),
-            pltpu.VMEM((1, count), jnp.int32),
-            pltpu.VMEM((1, count), jnp.int32),
-            pltpu.VMEM((1, count), jnp.int32),
             pltpu.VMEM((384, 1024), F32),
             pltpu.VMEM((n, 16, 128), jnp.int32),
             pltpu.VMEM((n, 16, 128), jnp.int32),
@@ -592,20 +615,17 @@
             pltpu.VMEM((4, 2, 5, 64, 128), BF16),
             pltpu.VMEM((4, 5, 64, 128), BF16),
             pltpu.VMEM((4, 5, 64, 128), BF16),
-            dma((5,)), dma, dma((n // GROUP,)),
+            dma((3,)), dma, dma((n // GROUP,)),
             dma((4, 5, 2)), dma((4, 5, 2)), dma((4, 2)), dma((4, 2)),
         ],
         compiler_params=pltpu.CompilerParams(
             collective_id=0, has_side_effects=True, vmem_limit_bytes=36 * 1024 * 1024
         ),
-    )(
-        state, lamb,
-        owner.reshape(1, count), element.reshape(1, count), shape_class.reshape(1, count), table,
-    )
+    )(state, lamb, key, table)
     new, source = pl.pallas_call(
         finish,
         out_shape=(jax.ShapeDtypeStruct(nodes, F32), jax.ShapeDtypeStruct((3000, 128), F32)),
-        in_specs=[vmem] * 5,
+        in_specs=[vmem] * 6,
         out_specs=(hbm, hbm),
         scratch_shapes=[pltpu.VMEM(nodes, F32), dma((6,))],
         compiler_params=pltpu.CompilerParams(vmem_limit_bytes=24 * 1024 * 1024),

time: 49 us -> 45.7 us (0.933)
  local copies, waits for them, and re-layouts: 5.88 us -> 3.85 us
  Pallas kernels: 41.7 us -> 40.2 us
  other arithmetic: 0 us -> 0.72 us
    unnamed x11 -> x5, local copies, waits for them, and re-layouts: 5.86 us -> 3.83 us
    pallas_call x1, Pallas kernels: 39.7 us -> 38.2 us  [body(): pl.pallas_call(functools.partial(kernel, nax, naz), out_shape=(jax.ShapeD...]
    add x0 -> x1, other arithmetic: none -> 0.72 us  [body(): key = ((element * 2 + shape_class) * n + owner[:, 0]).reshape(1, count)]
where the time goes in v2:
time: 45.7 us; the launch traced here: 45.4 us
  Pallas kernels  40.2 us (88%)
  local copies, waits for them, and re-layouts  3.85 us (8%)
  other arithmetic  0.72 us (2%)
  between operations  0.66 us (1%)
    pallas_call x1, Pallas kernels, body(): pl.pallas_call(functools.partial(kernel, nax, naz), out_shape=(jax.ShapeD...  38.2 us
    unnamed x5, local copies, waits for them, and re-layouts  3.83 us
    pallas_call x1, Pallas kernels, body(): pl.pallas_call(finish, out_shape=(jax.ShapeDtypeStruct(nodes, F32), jax.S...  2.02 us

profile of v2, /device:TPU:32, one launch (start us, length us, event | category | flops | bytes accessed | tf_op | source)
XLA Modules:
  0.0 45.4 jit_solution(5415492553355440608)
XLA Ops:
  0.6 0.7 %multiply_add_fusion = s32[256]{0:T(256)S(1)} fusion(s32[256]{0:T(256)} %bitcast.13, s32[256]{0:T(256)} %param.9, s32[256]{0:T(256)} %param.8), kind=kLoop, calls=%fused_computation | loop fusion | flops 1024 | bytes 4096 | tf_op jit(solution)/shard_map/add | solution.py:594
  1.3 1.0 %copy.9 = bf16[2,125,512]{2,1,0:T(8,128)(2,1)S(1)} copy(bf16[2,125,512]{2,0,1:T(2,128)(2,1)} %bitcast.12) | data formatting | bytes 512000
  2.4 0.0 copy-start
  2.4 1.7 %copy-done = f32[5,125,2,4,128]{4,3,2,1,0:T(4,128)S(1)} copy-done((f32[5,125,2,4,128]{4,3,2,1,0:T(4,128)S(1)}, f32[5,125,2,4,128]{4,3,2,1,0:T(4,128)}, u32[]{:S(2)}) %copy-start) | copy-done | bytes 2560024
  4.1 0.0 copy-start.1
  4.1 1.1 %copy-done.1 = bf16[256,3,512]{2,0,1:T(8,128)(2,1)S(1)} copy-done((bf16[256,3,512]{2,0,1:T(8,128)(2,1)S(1)}, bf16[256,3,512]{2,0,1:T(8,128)(2,1)}, u32[]{:S(2)}) %copy-start.1) | copy-done | bytes 786456
  5.2 38.2 %shard_map.77 = (f32[5,5,5,5,8,128]{5,4,3,2,1,0:T(8,128)S(1)}, f32[5,5,5,5,8,128]{5,4,3,2,1,0:T(8,128)S(1)}, f32[5,5,5,5,8,128]{5,4,3,2,1,0:T(8,128)S(1)}, f32[3...) custom-call(f32[5,5,5,5,8,128]{5,4,3,2,1,0:T(8,128)S(1)} %bitcast.8, ...), custom_call_target="tpu_custom_call" | custom-call | tf_op jit(solution)/shard_map/pallas_call | solution.py:597
  43.4 2.0 %shard_map.78 = (f32[5,5,5,5,8,128]{5,4,3,2,1,0:T(8,128)}, f32[3000,128]{1,0:T(8,128)}) custom-call(f32[5,5,5,5,8,128]{5,4,3,2,1,0:T(8,128)S(1)} %get-tuple-element.10.nxt, f32[5,5,5,5,8,128]{5,4,3,2,1,0:T(8,128)S(1)} %get-tuple-element.11.cur, f32[5,5,5,5,8,128]{5,4,3,2,1,0:T(8,128)S(1)} %get-tuple-element.12.acc, f32[3000,128]{1,0:T(8,128)S(1)} %get-tuple-element.13.s_ref, ...), custom_call_target="tpu_custom_call" | custom-call | tf_op jit(solution)/shard_map/pallas_call | solution.py:625
  (1 shorter events, 0.0 us)
Async XLA Ops:
  2.4 1.7 %copy-start = (f32[5,125,2,4,128]{4,3,2,1,0:T(4,128)S(1)}, f32[5,125,2,4,128]{4,3,2,1,0:T(4,128)}, u32[]{:S(2)}) copy-start(f32[5,125,2,4,128]{4,3,2,1,0:T(4,128)} %param.11) | copy-start | bytes 7680004
  4.1 1.1 %copy-start.1 = (bf16[256,3,512]{2,0,1:T(8,128)(2,1)S(1)}, bf16[256,3,512]{2,0,1:T(8,128)(2,1)}, u32[]{:S(2)}) copy-start(bf16[256,3,512]{2,0,1:T(8,128)(2,1)} %param.6) | copy-start | bytes 2359300

commit v3 on v2

--- a/solution.py
+++ b/solution.py
@@ -310,7 +310,7 @@
     pl.semaphore_wait(barrier, n - 1)
 
     def mail_out(i, carry):
-        other = lax.rem(me + i, n)
+        other = lax.rem(me + 37 * i, n)
         pltpu.make_async_remote_copy(
             src_ref=post.at[other, pl.ds(0, MAIL)], dst_ref=inbox.at[i, pl.ds(0, MAIL)],
             send_sem=mail_send, recv_sem=mail_recv.at[i // GROUP],
@@ -427,6 +427,9 @@
             left, right = unpack_faces(xl, (k, b), 7), unpack_faces(xr, (k, b), 7)
             for r in range(5):
                 def emit(f, a, total):
+                    if k == 0 and f in (1, 2, 3):
+                        at = ((f - 1) * 125 + a * 25 + b * 5 + r) * 8
+                        total = total + s_ref[pl.ds(pl.multiple_of(at, 8), 8), :]
                     total = scale * total
                     nxt[f, a, b, r] = total
                     acc[f, a, b, r] = acc[f, a, b, r] + total
@@ -508,19 +511,6 @@
                         128 * c:128 * c + 125, 128 * h:128 * h + 128
                     ]
 
-    def add_source(nxt):
-        def body(i, carry):
-            for j in range(25):
-                a, b, r = i, j // 5, j % 5
-                for c in range(3):
-                    at = (c * 125 + i * 25 + j) * 8
-                    nxt[c + 1, a, b, r] = (
-                        nxt[c + 1, a, b, r] + s_ref[pl.ds(pl.multiple_of(at, 8), 8), :]
-                    )
-            return carry
-
-        lax.fori_loop(0, 5, body, 0)
-
     for k in range(4):
         cur, nxt = (even, odd) if k % 2 == 0 else (odd, even)
         z_pass(cur, nxt)
@@ -529,7 +519,6 @@
             gather_first()
             lax.fori_loop(1, groups - 1, gather, 0)
             gather_last()
-            add_source(nxt)
         if k < 3:
             x_pass(cur, nxt, k, DT / (k + 1))
 

time: 45.7 us -> 44.9 us (0.982)
  Pallas kernels: 40.2 us -> 39.5 us
    pallas_call x1, Pallas kernels: 38.2 us -> 37.5 us  [body(): pl.pallas_call(functools.partial(kernel, nax, naz), out_shape=(jax.ShapeD...]
where the time goes in v3:
time: 44.9 us; the launch traced here: 44.7 us
  Pallas kernels  39.5 us (88%)
  local copies, waits for them, and re-layouts  3.85 us (9%)
  other arithmetic  0.72 us (2%)
  between operations  0.66 us (1%)
    pallas_call x1, Pallas kernels, body(): pl.pallas_call(functools.partial(kernel, nax, naz), out_shape=(jax.ShapeD...  37.5 us
    unnamed x5, local copies, waits for them, and re-layouts  3.83 us
    pallas_call x1, Pallas kernels, body(): pl.pallas_call(finish, out_shape=(jax.ShapeDtypeStruct(nodes, F32), jax.S...  2.02 us

profile of v3, /device:TPU:32, one launch (start us, length us, event | category | flops | bytes accessed | tf_op | source)
XLA Modules:
  0.0 44.7 jit_solution(16771555976738919664)
XLA Ops:
  0.6 0.7 %multiply_add_fusion = s32[256]{0:T(256)S(1)} fusion(s32[256]{0:T(256)} %bitcast.13, s32[256]{0:T(256)} %param.9, s32[256]{0:T(256)} %param.8), kind=kLoop, calls=%fused_computation | loop fusion | flops 1024 | bytes 4096 | tf_op jit(solution)/shard_map/add | solution.py:583
  1.3 1.0 %copy.9 = bf16[2,125,512]{2,1,0:T(8,128)(2,1)S(1)} copy(bf16[2,125,512]{2,0,1:T(2,128)(2,1)} %bitcast.12) | data formatting | bytes 512000
  2.4 0.0 copy-start
  2.4 1.7 %copy-done = f32[5,125,2,4,128]{4,3,2,1,0:T(4,128)S(1)} copy-done((f32[5,125,2,4,128]{4,3,2,1,0:T(4,128)S(1)}, f32[5,125,2,4,128]{4,3,2,1,0:T(4,128)}, u32[]{:S(2)}) %copy-start) | copy-done | bytes 2560024
  4.1 0.0 copy-start.1
  4.1 1.1 %copy-done.1 = bf16[256,3,512]{2,0,1:T(8,128)(2,1)S(1)} copy-done((bf16[256,3,512]{2,0,1:T(8,128)(2,1)S(1)}, bf16[256,3,512]{2,0,1:T(8,128)(2,1)}, u32[]{:S(2)}) %copy-start.1) | copy-done | bytes 786456
  5.2 37.5 %shard_map.77 = (f32[5,5,5,5,8,128]{5,4,3,2,1,0:T(8,128)S(1)}, f32[5,5,5,5,8,128]{5,4,3,2,1,0:T(8,128)S(1)}, f32[5,5,5,5,8,128]{5,4,3,2,1,0:T(8,128)S(1)}, f32[3...) custom-call(f32[5,5,5,5,8,128]{5,4,3,2,1,0:T(8,128)S(1)} %bitcast.8, ...), custom_call_target="tpu_custom_call" | custom-call | tf_op jit(solution)/shard_map/pallas_call | solution.py:586
  42.7 2.0 %shard_map.78 = (f32[5,5,5,5,8,128]{5,4,3,2,1,0:T(8,128)}, f32[3000,128]{1,0:T(8,128)}) custom-call(f32[5,5,5,5,8,128]{5,4,3,2,1,0:T(8,128)S(1)} %get-tuple-element.10.nxt, f32[5,5,5,5,8,128]{5,4,3,2,1,0:T(8,128)S(1)} %get-tuple-element.11.cur, f32[5,5,5,5,8,128]{5,4,3,2,1,0:T(8,128)S(1)} %get-tuple-element.12.acc, f32[3000,128]{1,0:T(8,128)S(1)} %get-tuple-element.13.s_ref, ...), custom_call_target="tpu_custom_call" | custom-call | tf_op jit(solution)/shard_map/pallas_call | solution.py:614
  (1 shorter events, 0.0 us)
Async XLA Ops:
  2.4 1.7 %copy-start = (f32[5,125,2,4,128]{4,3,2,1,0:T(4,128)S(1)}, f32[5,125,2,4,128]{4,3,2,1,0:T(4,128)}, u32[]{:S(2)}) copy-start(f32[5,125,2,4,128]{4,3,2,1,0:T(4,128)} %param.11) | copy-start | bytes 7680004
  4.1 1.1 %copy-start.1 = (bf16[256,3,512]{2,0,1:T(8,128)(2,1)S(1)}, bf16[256,3,512]{2,0,1:T(8,128)(2,1)}, u32[]{:S(2)}) copy-start(bf16[256,3,512]{2,0,1:T(8,128)(2,1)} %param.6) | copy-start | bytes 2359300

commit v4 on v3

--- a/solution.py
+++ b/solution.py
@@ -15,7 +15,7 @@
 LIFT = 10.0
 VOLUME = 2.0
 MAIL = 9
-GROUP = 16
+GROUP = 32
 MESH = pl.DeviceIdType.MESH
 F32 = jnp.float32
 BF16 = jnp.bfloat16

time: 44.9 us -> 45.1 us (level)
  no operation moved by 1% of the time
where the time goes in v4:
time: 45.1 us; the launch traced here: 44.8 us
  Pallas kernels  39.6 us (88%)
  local copies, waits for them, and re-layouts  3.85 us (9%)
  other arithmetic  0.72 us (2%)
  between operations  0.66 us (1%)
    pallas_call x1, Pallas kernels, body(): pl.pallas_call(functools.partial(kernel, nax, naz), out_shape=(jax.ShapeD...  37.6 us
    unnamed x5, local copies, waits for them, and re-layouts  3.83 us
    pallas_call x1, Pallas kernels, body(): pl.pallas_call(finish, out_shape=(jax.ShapeDtypeStruct(nodes, F32), jax.S...  2.02 us

profile of v4, /device:TPU:32, one launch (start us, length us, event | category | flops | bytes accessed | tf_op | source)
XLA Modules:
  0.0 44.8 jit_solution(17245759960586174370)
XLA Ops:
  0.6 0.7 %multiply_add_fusion = s32[256]{0:T(256)S(1)} fusion(s32[256]{0:T(256)} %bitcast.13, s32[256]{0:T(256)} %param.9, s32[256]{0:T(256)} %param.8), kind=kLoop, calls=%fused_computation | loop fusion | flops 1024 | bytes 4096 | tf_op jit(solution)/shard_map/add | solution.py:583
  1.3 1.0 %copy.9 = bf16[2,125,512]{2,1,0:T(8,128)(2,1)S(1)} copy(bf16[2,125,512]{2,0,1:T(2,128)(2,1)} %bitcast.12) | data formatting | bytes 512000
  2.4 0.0 copy-start
  2.4 1.7 %copy-done = f32[5,125,2,4,128]{4,3,2,1,0:T(4,128)S(1)} copy-done((f32[5,125,2,4,128]{4,3,2,1,0:T(4,128)S(1)}, f32[5,125,2,4,128]{4,3,2,1,0:T(4,128)}, u32[]{:S(2)}) %copy-start) | copy-done | bytes 2560024
  4.1 0.0 copy-start.1
  4.1 1.1 %copy-done.1 = bf16[256,3,512]{2,0,1:T(8,128)(2,1)S(1)} copy-done((bf16[256,3,512]{2,0,1:T(8,128)(2,1)S(1)}, bf16[256,3,512]{2,0,1:T(8,128)(2,1)}, u32[]{:S(2)}) %copy-start.1) | copy-done | bytes 786456
  5.2 37.6 %shard_map.77 = (f32[5,5,5,5,8,128]{5,4,3,2,1,0:T(8,128)S(1)}, f32[5,5,5,5,8,128]{5,4,3,2,1,0:T(8,128)S(1)}, f32[5,5,5,5,8,128]{5,4,3,2,1,0:T(8,128)S(1)}, f32[3...) custom-call(f32[5,5,5,5,8,128]{5,4,3,2,1,0:T(8,128)S(1)} %bitcast.8, ...), custom_call_target="tpu_custom_call" | custom-call | tf_op jit(solution)/shard_map/pallas_call | solution.py:586
  42.8 2.0 %shard_map.78 = (f32[5,5,5,5,8,128]{5,4,3,2,1,0:T(8,128)}, f32[3000,128]{1,0:T(8,128)}) custom-call(f32[5,5,5,5,8,128]{5,4,3,2,1,0:T(8,128)S(1)} %get-tuple-element.10.nxt, f32[5,5,5,5,8,128]{5,4,3,2,1,0:T(8,128)S(1)} %get-tuple-element.11.cur, f32[5,5,5,5,8,128]{5,4,3,2,1,0:T(8,128)S(1)} %get-tuple-element.12.acc, f32[3000,128]{1,0:T(8,128)S(1)} %get-tuple-element.13.s_ref, ...), custom_call_target="tpu_custom_call" | custom-call | tf_op jit(solution)/shard_map/pallas_call | solution.py:614
  (1 shorter events, 0.0 us)
Async XLA Ops:
  2.4 1.7 %copy-start = (f32[5,125,2,4,128]{4,3,2,1,0:T(4,128)S(1)}, f32[5,125,2,4,128]{4,3,2,1,0:T(4,128)}, u32[]{:S(2)}) copy-start(f32[5,125,2,4,128]{4,3,2,1,0:T(4,128)} %param.11) | copy-start | bytes 7680004
  4.1 1.1 %copy-start.1 = (bf16[256,3,512]{2,0,1:T(8,128)(2,1)S(1)}, bf16[256,3,512]{2,0,1:T(8,128)(2,1)}, u32[]{:S(2)}) copy-start(bf16[256,3,512]{2,0,1:T(8,128)(2,1)} %param.6) | copy-start | bytes 2359300
